TPU v7x, 256 devices: a whole 4x4x8 slice. The times are simulated.
256 devices in a mesh: tensor: 32 (over x, z), context: 2 (over core), dp: 4 (over y).
Axes of the slice: x: 4, y: 4, z: 8, core: 2. Of those that a mesh axis runs over, the one named last changes fastest.
Arguments:
- hidden_prev: bfloat16 [1024, 7168], P(('context', 'dp'), 'tensor'), may hold values from -300 to 300
- next_ids: int32 [1024], P(('context', 'dp')), may hold values from 0 to 65535
- targets: int32 [1024], P(('context', 'dp')), may hold values from 0 to 65535
- loss_mask: int32 [1024], P(('context', 'dp')), may hold values from 0 to 1, as said below
- gain_hidden: bfloat16 [7168], P('tensor'), may hold values from 0.099609375 to 1.8984375
- gain_embed: bfloat16 [7168], P('tensor'), may hold values from 0.099609375 to 1.8984375
- gain_final: bfloat16 [7168], P(('context', 'dp')), may hold values from 0.099609375 to 1.8984375
- embed_table: bfloat16 [65536, 7168], P(('context', 'dp'), 'tensor'), may hold values from -200 to 200
- proj_hidden: bfloat16 [7168, 7168], P('tensor', ('context', 'dp')), may hold values from -0.046875 to 0.046875
- proj_embed: bfloat16 [7168, 7168], P('tensor', ('context', 'dp')), may hold values from -0.046875 to 0.046875
- head_weight: bfloat16 [7168, 65536], P(('context', 'dp'), 'tensor'), may hold values from -8 to 8
Outputs:
- loss_value: float32 [], replicated
- hidden_grad: bfloat16 [1024, 7168], P(('context', 'dp'), 'tensor')
- proj_hidden_grad: bfloat16 [7168, 7168], P('tensor', ('context', 'dp'))
- proj_embed_grad: bfloat16 [7168, 7168], P('tensor', ('context', 'dp'))
- head_grad: bfloat16 [7168, 65536], P(('context', 'dp'), 'tensor')
Inputs may be any that keep to these rules, and one draw needn't show every extreme that they name: `loss_mask`: the last token always counts.
All inputs are finite; a program needn't handle non-finite values.
Results may differ from a plain program's by a relative error of at most 0.011.
The roundings to bfloat16 on the way count: a program that leaves them out, or rounds other values in their place, can miss the bound.
Values may be sent and summed in bfloat16 or wider, within the bound.
A program may use at most 128 MiB of HBM per device.

v0:
```python
import jax
import jax.numpy as jnp
from jax import lax
from jax.sharding import PartitionSpec as P

D = 7168


EPS = 1e-06


def scale_rows(squares):
    return jnp.sqrt(squares / D + EPS)[:, None]


def per_device(
    hidden_prev,
    next_ids,
    targets,
    loss_mask,
    gain_hidden,
    gain_embed,
    gain_final,
    embed_table,
    proj_hidden,
    proj_embed,
    head_weight,
):
    mask_weights = loss_mask.astype(jnp.float32)
    mask_total = lax.psum(jnp.sum(mask_weights), ("context", "dp"))
    hidden = hidden_prev.astype(jnp.float32)
    hidden_squares = jnp.sum(hidden * hidden, axis=1)
    gain_hid = gain_hidden.astype(jnp.float32)
    gain_emb = gain_embed.astype(jnp.float32)
    gain_fin = gain_final.astype(jnp.float32)
    every_id = lax.all_gather(next_ids, ("context", "dp"), axis=0, tiled=True)
    table_rows = embed_table.shape[0]
    local_ids = every_id - lax.axis_index(("context", "dp")) * table_rows
    inside = (local_ids >= 0) & (local_ids < table_rows)
    looked_up = jnp.take(embed_table, jnp.clip(local_ids, 0, table_rows - 1), axis=0).astype(
        jnp.float32
    )
    embed_terms = jnp.where(inside[:, None], looked_up, jnp.float32(0.0))
    hidden_total = lax.psum(hidden_squares, "tensor")
    hidden_rms = scale_rows(hidden_total)
    hidden_unit = hidden / hidden_rms
    own_hidden = (hidden_unit * gain_hid).astype(jnp.bfloat16)
    normed_hidden = lax.all_gather(own_hidden, ("context", "dp"), axis=0, tiled=True)
    embedded = lax.psum(embed_terms.astype(jnp.bfloat16), ("context", "dp")).astype(jnp.float32)
    embed_total = lax.psum(jnp.sum(embedded * embedded, axis=1), "tensor")
    normed_embed = (embedded / scale_rows(embed_total) * gain_emb).astype(jnp.bfloat16)
    mixed_terms = jnp.dot(normed_hidden, proj_hidden, preferred_element_type=jnp.float32) + jnp.dot(
        normed_embed, proj_embed, preferred_element_type=jnp.float32
    )
    mixed = lax.psum(mixed_terms, "tensor")
    mixed_rms = scale_rows(lax.psum(jnp.sum(mixed * mixed, axis=1), ("context", "dp")))
    mixed_unit = mixed / mixed_rms
    final_normed = (mixed_unit * gain_fin).astype(jnp.bfloat16)
    logits = lax.psum_scatter(
        jnp.dot(final_normed, head_weight, preferred_element_type=jnp.float32),
        ("context", "dp"),
        scatter_dimension=0,
        tiled=True,
    )
    vocab_cols = head_weight.shape[1]
    columns = (
        lax.broadcasted_iota(jnp.int32, (1, vocab_cols), 1) + lax.axis_index("tensor") * vocab_cols
    )
    target_hits = columns == targets[:, None]
    target_logit = jnp.sum(jnp.where(target_hits, logits, jnp.float32(0.0)), axis=1)
    local_top = jnp.max(logits, axis=1)
    row_top = lax.pmax(local_top, "tensor")
    local_total = jnp.sum(jnp.exp(logits - row_top[:, None]), axis=1)
    exp_total, picked = lax.psum((local_total, target_logit), "tensor")
    log_total = row_top + jnp.log(exp_total)
    loss_value = (
        lax.psum(jnp.sum(mask_weights * (log_total - picked)), ("context", "dp")) / mask_total
    )
    probs = jnp.exp(logits - log_total[:, None])
    logit_grad = (
        (mask_weights / mask_total)[:, None] * (probs - target_hits.astype(jnp.float32))
    ).astype(jnp.bfloat16)
    every_grad = lax.all_gather(logit_grad, ("context", "dp"), axis=0, tiled=True)
    head_grad = lax.dot_general(
        final_normed, every_grad, (((0,), (0,)), ((), ())), preferred_element_type=jnp.float32
    ).astype(jnp.bfloat16)
    final_terms = lax.dot_general(
        every_grad, head_weight, (((1,), (1,)), ((), ())), preferred_element_type=jnp.float32
    )
    final_grad = lax.psum(final_terms, "tensor")
    scaled = final_grad * gain_fin
    inner = lax.psum(jnp.sum(scaled * mixed_unit, axis=1), ("context", "dp"))
    mixed_grad = ((scaled - mixed_unit * (inner / D)[:, None]) / mixed_rms).astype(jnp.bfloat16)
    proj_hidden_grad = lax.dot_general(
        normed_hidden, mixed_grad, (((0,), (0,)), ((), ())), preferred_element_type=jnp.float32
    ).astype(jnp.bfloat16)
    proj_embed_grad = lax.dot_general(
        normed_embed, mixed_grad, (((0,), (0,)), ((), ())), preferred_element_type=jnp.float32
    ).astype(jnp.bfloat16)
    normed_hidden_grad = lax.psum_scatter(
        lax.dot_general(
            mixed_grad, proj_hidden, (((1,), (1,)), ((), ())), preferred_element_type=jnp.float32
        ),
        ("context", "dp"),
        scatter_dimension=0,
        tiled=True,
    )
    scaled_hidden = normed_hidden_grad * gain_hid
    inner_hidden = lax.psum(jnp.sum(scaled_hidden * hidden_unit, axis=1), "tensor")
    hidden_grad = ((scaled_hidden - hidden_unit * (inner_hidden / D)[:, None]) / hidden_rms).astype(
        jnp.bfloat16
    )
    return (loss_value, hidden_grad, proj_hidden_grad, proj_embed_grad, head_grad)


def solution(mesh):
    return jax.shard_map(
        per_device,
        mesh=mesh,
        in_specs=(
            P(("context", "dp"), "tensor"),
            P(("context", "dp")),
            P(("context", "dp")),
            P(("context", "dp")),
            P("tensor"),
            P("tensor"),
            P(("context", "dp")),
            P(("context", "dp"), "tensor"),
            P("tensor", ("context", "dp")),
            P("tensor", ("context", "dp")),
            P(("context", "dp"), "tensor"),
        ),
        out_specs=(
            P(),
            P(("context", "dp"), "tensor"),
            P("tensor", ("context", "dp")),
            P("tensor", ("context", "dp")),
            P(("context", "dp"), "tensor"),
        ),
        check_vma=False,
    )
```

profile of v0, /device:TPU:1, one launch (start us, length us, event | category | flops | bytes accessed | tf_op | source)
XLA Modules:
  0.0 972.4 jit_solution(17096561062931674885)
XLA Ops:
  7.2 0.0 copy-start
  7.2 0.0 all-reduce.7.cloned.1.call-start
  7.2 15.9 %all-gather = s32[8,1,128]{2,1,0:T(1,128)S(1)} all-gather(s32[1,1,128]{2,1,0:T(1,128)} %bitcast.25), channel_id=1, replica_groups=mesh['tensor'=32,'context'=2,'dp'=4] {'context','dp'}, dimensions={0}, use_global_device_ids=true | all-gather | bytes 4608 | tf_op jit(solution)/shard_map/all_gather | solution.py:36
  23.1 6.3 copy.19
  29.4 0.0 copy-start.7
  29.4 0.0 copy-start.8
  29.4 0.0 copy-start.1
  29.4 6.2 gather_fusion
  35.7 1.1 select_convert_fusion
  36.8 0.0 all-reduce.7.cloned.1.call-update
  36.8 0.0 all-reduce.9.cloned.1.call-start
  36.9 0.0 copy-done.7
  36.9 0.0 copy-done.8
  36.9 0.0 copy-done.1
  37.0 64.7 %all-reduce.7.cloned.1.call-done = bf16[1024,224]{1,0:T(8,128)(2,1)} async-done(((bf16[1024,224]{1,0:T(8,128)(2,1)}), bf16[1024,224]{1,0:T(8,128)(2,1)}) %all-reduce.7.cloned.1.call-update) | async-done | bytes 458768 | tf_op jit(solution)/shard_map/psum | solution.py:49
  101.7 1.3 fusion
  103.0 62.0 %all-reduce.1 = (f32[1024]{0:T(1024)S(1)}, f32[128]{0:T(128)S(1)}) all-reduce(f32[1024]{0:T(1024)S(1)} %fusion, f32[128]{0:T(128)S(1)} %fusion.8), channel_id=1, replica_groups=mesh['tensor'=32,'context'=2,'dp'=4] {'tensor'}, use_global_device_ids=true, to_apply=%region_4.5 | all-reduce | flops 1152 | bytes 9216 | tf_op jit(solution)/shard_map/psum | solution.py:50
  165.0 0.1 multiply_convert_fusion.3
  165.1 38.3 %all_gather.9 = bf16[1024,224]{0,1:T(8,128)(2,1)S(1)} all-gather(bf16[128,224]{0,1:T(8,128)(2,1)S(1)} %multiply_convert_fusion.3), channel_id=1, replica_groups=mesh['tensor'=32,'context'=2,'dp'=4] {'context','dp'}, dimensions={0}, use_global_device_ids=true | all-gather | bytes 516096 | tf_op jit(solution)/shard_map/all_gather | solution.py:48
  203.4 0.0 copy-done.6
  203.4 1.8 fusion.11
  205.2 0.0 copy-done
  205.2 2.6 convolution_add_fusion
  207.8 0.0 all-reduce.9.cloned.1.call-update
  207.8 0.0 reduce-scatter.3.cloned.1.call-start
  207.8 0.6 copy-done.4
  208.5 149.1 %all-reduce.9.cloned.1.call-done = f32[1024,896]{1,0:T(8,128)} async-done(((f32[1024,896]{1,0:T(8,128)}), f32[1024,896]{1,0:T(8,128)}) %all-reduce.9.cloned.1.call-update) | async-done | bytes 3670032 | tf_op jit(solution)/shard_map/psum | solution.py:55
  357.6 2.3 multiply_reduce_fusion.1
  359.9 18.3 %psum.88 = f32[1024]{0:T(1024)S(1)} all-reduce(f32[1024]{0:T(1024)S(1)} %multiply_reduce_fusion.1), channel_id=1, replica_groups=mesh['tensor'=32,'context'=2,'dp'=4] {'context','dp'}, use_global_device_ids=true, to_apply=%region_7.8 | all-reduce | flops 1024 | bytes 8192 | tf_op jit(solution)/shard_map/psum | solution.py:56
  378.2 10.9 %fusion.7 = f32[1024,2048]{1,0:T(8,128)} fusion(bf16[896,2048]{1,0:T(8,128)(2,1)} %param.21, f32[896]{0:T(1024)S(1)} %convert_element_type.63, f32[1024,896]{1,0:T(8,128)} %all-reduce.9.cloned.1.call-done, f32[1024]{0:T(1024)S(1)} %add_sqrt_fusion), kind=kOutput, calls=%fused_computation.23 | convolution fusion | flops 3760848896 | bytes 15736320 | tf_op jit(solution)/shard_map/dot_general | solution.py:60
  389.2 0.0 reduce-scatter.3.cloned.1.call-update
  389.2 0.0 all-gather.3.cloned.1.call-start
  389.3 89.7 %reduce-scatter.3.cloned.1.call-done = f32[128,2048]{1,0:T(8,128)} async-done(((f32[1024,2048]{1,0:T(8,128)}), f32[128,2048]{1,0:T(8,128)}) %reduce-scatter.3.cloned.1.call-update) | async-done | bytes 1048592 | tf_op jit(solution)/shard_map/reduce_scatter | solution.py:59
  479.0 1.4 reduce_max.9
  480.4 61.0 %pmax.7 = f32[128]{0:T(128)S(1)} all-reduce(f32[128]{0:T(128)S(1)} %reduce_max.9), channel_id=1, replica_groups=mesh['tensor'=32,'context'=2,'dp'=4] {'tensor'}, use_global_device_ids=true, to_apply=%region_10.11 | all-reduce | flops 128 | bytes 1024 | tf_op jit(solution)/shard_map/pmax | solution.py:72
  541.4 0.0 copy-done.3
  541.4 1.6 fusion.3
  543.0 55.7 %all-reduce = (f32[128]{0:T(128)S(1)}, f32[128]{0:T(128)S(1)}) all-reduce(f32[128]{0:T(128)S(1)} %get-tuple-element.6, f32[128]{0:T(128)S(1)} %get-tuple-element.5), channel_id=1, replica_groups=mesh['tensor'=32,'context'=2,'dp'=4] {'tensor'}, use_global_device_ids=true, to_apply=%region_12.13 | all-reduce | flops 256 | bytes 2048 | tf_op jit(solution)/shard_map/psum | solution.py:74
  598.7 0.0 copy-done.5
  598.7 0.6 convert_reduce_fusion
  599.3 42.1 %psum.92 = f32[]{:T(128)} all-reduce(f32[]{:T(128)} %get-tuple-element.7), channel_id=1, replica_groups=mesh['tensor'=32,'context'=2,'dp'=4] {'context','dp'}, use_global_device_ids=true, to_apply=%region_18.19 | all-reduce | flops 1 | bytes 8 | tf_op jit(solution)/shard_map/psum | solution.py:30
  641.4 0.6 convert_divide_fusion.2
  642.0 2.4 fusion.6
  644.5 0.0 all-gather.3.cloned.1.call-update
  644.5 0.0 all-reduce.11.cloned.1.call-start
  644.5 28.6 %all-gather.3.cloned.1.call-done = bf16[1024,2048]{1,0:T(8,128)(2,1)} async-done(((bf16[128,2048]{1,0:T(8,128)(2,1)}), bf16[1024,2048]{1,0:T(8,128)(2,1)}) %all-gather.3.cloned.1.call-update) | async-done | bytes 4194320 | tf_op jit(solution)/shard_map/all_gather | solution.py:83
  673.1 9.7 fusion.13
  682.8 0.0 all-reduce.11.cloned.1.call-update
  682.8 0.2 reduce-scatter.5.cloned.1.call-start
  683.0 157.4 %all-reduce.11.cloned.1.call-done = f32[1024,896]{1,0:T(8,128)} async-done(((f32[1024,896]{1,0:T(8,128)}), f32[1024,896]{1,0:T(8,128)}) %all-reduce.11.cloned.1.call-update) | async-done | bytes 3670032 | tf_op jit(solution)/shard_map/psum | solution.py:90
  840.5 3.8 multiply_reduce_fusion
  844.3 19.2 %all-reduce.2 = (f32[]{:T(128)}, f32[1024]{0:T(1024)S(1)}) all-reduce(f32[]{:T(128)} %get-tuple-element.8, f32[1024]{0:T(1024)S(1)} %multiply_reduce_fusion), channel_id=1, replica_groups=mesh['tensor'=32,'context'=2,'dp'=4] {'context','dp'}, use_global_device_ids=true, to_apply=%region_16.17 | all-reduce | flops 1025 | bytes 8200 | tf_op jit(solution)/shard_map/psum | solution.py:77
  863.4 3.6 divide_convert_fusion
  867.1 1.7 fusion.14
  868.8 0.0 reduce-scatter.5.cloned.1.call-update
  868.8 0.0 copy-start.2
  868.8 9.4 convolution_convert_fusion
  879.5 1.4 convolution_convert_fusion.2
  880.9 0.0 copy-done.2
  880.9 1.6 convolution_convert_fusion.1
  882.5 18.1 %reduce-scatter.5.cloned.1.call-done = f32[128,224]{0,1:T(8,128)} async-done(((f32[1024,224]{0,1:T(8,128)}), f32[128,224]{0,1:T(8,128)}) %reduce-scatter.5.cloned.1.call-update) | async-done | bytes 114704 | tf_op jit(solution)/shard_map/reduce_scatter | solution.py:100
  900.6 1.0 multiply_reduce_fusion.2
  901.6 61.1 %psum.95 = f32[128]{0:T(128)S(1)} all-reduce(f32[128]{0:T(128)S(1)} %multiply_reduce_fusion.2), channel_id=1, replica_groups=mesh['tensor'=32,'context'=2,'dp'=4] {'tensor'}, use_global_device_ids=true, to_apply=%region_24.25 | all-reduce | flops 128 | bytes 1024 | tf_op jit(solution)/shard_map/psum | solution.py:109
  962.8 1.6 divide_convert_fusion.1
  (17 shorter events, 0.1 us)
Async XLA Ops:
  7.2 198.0 %copy-start = (bf16[224,896]{1,0:T(8,128)(2,1)S(1)}, bf16[224,896]{1,0:T(8,128)(2,1)}, u32[]{:S(2)}) copy-start(bf16[224,896]{1,0:T(8,128)(2,1)} %param.19) | copy-start | bytes 1204228
  7.2 94.5 %all-reduce.7.cloned.1.call-start = ((), (), s32[]{:S(2)}) async-start(), calls=%async_computation.2 | async-start | bytes 1048576 | tf_op jit(solution)/shard_map/psum | solution.py:49
  29.4 7.5 copy-start.7
  29.4 7.5 copy-start.8
  29.4 7.5 copy-start.1
  29.4 173.9 %copy-start.6 = (bf16[224,896]{1,0:T(8,128)(2,1)S(1)}, bf16[224,896]{1,0:T(8,128)(2,1)}, u32[]{:S(2)}) copy-start(bf16[224,896]{1,0:T(8,128)(2,1)} %param.20) | copy-start | bytes 1204228
  36.8 320.8 %all-reduce.9.cloned.1.call-start = ((), (), s32[]{:S(2)}) async-start(), calls=%async_computation.3 | async-start | bytes 7340032 | tf_op jit(solution)/shard_map/psum | solution.py:55
  207.8 0.7 copy-start.4
  207.8 271.2 %reduce-scatter.3.cloned.1.call-start = ((), (), s32[]{:S(2)}) async-start(), calls=%async_computation.4 | async-start | bytes 9437184 | tf_op jit(solution)/shard_map/reduce_scatter | solution.py:59
  389.2 152.2 %copy-start.3 = (s32[128]{0:T(128)S(1)}, s32[128]{0:T(128)}, u32[]{:S(2)}) copy-start(s32[128]{0:T(128)} %param.13) | copy-start | bytes 1540
  389.2 209.5 %copy-start.5 = (s32[128]{0:T(128)S(1)}, s32[128]{0:T(128)}, u32[]{:S(2)}) copy-start(s32[128]{0:T(128)} %param.14) | copy-start | bytes 1540
  389.2 283.9 %all-gather.3.cloned.1.call-start = ((), (), s32[]{:S(2)}) async-start(), calls=%async_computation.5 | async-start | bytes 4718592 | tf_op jit(solution)/shard_map/all_gather | solution.py:83
  644.5 196.0 %all-reduce.11.cloned.1.call-start = ((), (), s32[]{:S(2)}) async-start(), calls=%async_computation.6 | async-start | bytes 7340032 | tf_op jit(solution)/shard_map/psum | solution.py:90
  682.8 217.8 %reduce-scatter.5.cloned.1.call-start = ((), (), s32[]{:S(2)}) async-start(), calls=%async_computation.7 | async-start | bytes 1032192 | tf_op jit(solution)/shard_map/reduce_scatter | solution.py:100
  868.8 12.1 %copy-start.2 = (bf16[1024,224]{1,0:T(8,128)(2,1)S(1)}, bf16[1024,224]{1,0:T(8,128)(2,1)}, u32[]{:S(2)}) copy-start(bf16[1024,224]{1,0:T(8,128)(2,1)} %all-reduce.7.cloned.1.call-done) | copy-start | bytes 1376260
Sparse Core Ops, SparseCore 0:
  36.9 64.7 all-reduce.6
  207.9 149.6 all-reduce.8
  389.3 89.6 reduce-scatter.2
  644.6 28.4 all-gather.2
  682.9 157.4 all-reduce.10
  868.9 31.6 reduce-scatter.4
where the time goes:
time: 984 us; the launch traced here: 972 us
  waiting for transfers between devices  508 us (52%)
  blocking collectives  373 us (38%)
  matrix products  39.1 us (4%)
  other arithmetic  21.6 us (2%)
  between operations  16.8 us (2%)
  local copies, waits for them, and re-layouts  13.1 us (1%)
    psum x1, waiting for transfers between devices, per_device(): final_grad = lax.psum(final_terms, 'tensor')  157 us
    psum x1, waiting for transfers between devices, per_device(): mixed = lax.psum(mixed_terms, 'tensor')  149 us
    reduce_scatter x1, waiting for transfers between devices, per_device(): lax.psum_scatter(jnp.dot(final_normed, head_weight, preferred_element_typ...  89.7 us
    psum x1, waiting for transfers between devices, per_device(): lax.psum(embed_terms.astype(jnp.bfloat16), ('context', 'dp'))  64.7 us
    psum x1, blocking collectives, per_device(): embed_total = lax.psum(jnp.sum(embedded * embedded, axis=1), 'tensor')  62 us
    psum x1, blocking collectives, per_device(): lax.psum(jnp.sum(scaled_hidden * hidden_unit, axis=1), 'tensor')  61.1 us
    pmax x1, blocking collectives, per_device(): row_top = lax.pmax(local_top, 'tensor')  61 us
    psum x1, blocking collectives, per_device(): exp_total, picked = lax.psum((local_total, target_logit), 'tensor')  55.7 us
  transfers between devices with their start and end apart: 6, of which 6 were waited for; matrix products, arithmetic and copies ran while one was open for 1% of the time, Pallas kernels for 0%

commit v1 on v0

v1 whole, which is shorter than its diff:
```python
import functools
import jax
import jax.numpy as jnp
from jax import lax
from jax.experimental import pallas as pl
from jax.experimental.pallas import tpu as pltpu
from jax.sharding import PartitionSpec as P

D = 7168
EPS = 1e-06
MESH = pl.DeviceIdType.MESH
F32 = jnp.float32
BF16 = jnp.bfloat16
NX, NZ, NC, NY = 4, 8, 2, 4
NT, NG = NX * NZ, NC * NY
ROWS = 32
OWN = 128
WIDE = 896
CA = 640
CB = WIDE - CA
FEAT = 224
VOC = 2048
TABLE = 8192
X_ORDER = (2, 1, 3)
Z_ORDER = (4, 3, 5, 2, 6, 1, 7)
VMEM_LIMIT = 60 * 1024 * 1024


def place():
    t = lax.axis_index("tensor")
    return t // NZ, t % NZ, lax.axis_index("context"), lax.axis_index("dp")


def rcopy(src, dst, ss, rs, dev):
    return pltpu.make_async_remote_copy(
        src_ref=src, dst_ref=dst, send_sem=ss, recv_sem=rs, device_id=dev, device_id_type=MESH
    )


def greet_all():
    x, z, c, y = place()
    t = x * NZ + z
    bar = pltpu.get_barrier_semaphore()

    def hello(k, carry):
        pl.semaphore_signal(
            bar, inc=1, device_id={"tensor": (t + k) % NT}, device_id_type=MESH
        )
        return carry

    lax.fori_loop(1, NT, hello, 0)
    for dc in range(NC):
        for dy in range(NY):
            if dc or dy:
                pl.semaphore_signal(
                    bar,
                    inc=1,
                    device_id={"context": (c + dc) % NC, "dp": (y + dy) % NY},
                    device_id_type=MESH,
                )
    pl.semaphore_wait(bar, NT - 1 + NG - 1)


def to_row(col):
    return jnp.broadcast_to(col, (OWN, OWN)).T[:1, :]


def to_col(row):
    return jnp.broadcast_to(row, (OWN, OWN)).T[:, :1]


def share_tensor(tile, recv, ss, rs):
    x, z, _, _ = place()
    t = x * NZ + z
    recv[t] = tile

    def send(k, carry):
        rcopy(recv.at[t], recv.at[t], ss, rs, {"tensor": (t + k) % NT}).start()
        return carry

    lax.fori_loop(1, NT, send, 0)
    every = rcopy(
        recv.at[pl.ds(0, NT - 1)], recv.at[pl.ds(0, NT - 1)], ss, rs, {"tensor": (t + 1) % NT}
    )
    every.wait_recv()
    every.wait_send()


def g_peers():
    _, _, c, y = place()
    for dy in (2, 1, 3, 0):
        for dc in (1, 0):
            if dc or dy:
                cb, yb = (c + dc) % NC, (y + dy) % NY
                yield cb * NY + yb, {"context": cb, "dp": yb}


def share_g(recv, ss, rs):
    _, _, c, y = place()
    g = c * NY + y
    copies = []
    for i, (_, dev) in enumerate(g_peers()):
        copy = rcopy(recv.at[g], recv.at[g], ss.at[i], rs.at[i], dev)
        copy.start()
        copies.append(copy)
    return copies


def scatter_g(src, recv, ss, rs):
    _, _, c, y = place()
    g = c * NY + y
    copies = []
    for i, (gb, dev) in enumerate(g_peers()):
        copy = rcopy(src.at[gb], recv.at[g], ss.at[i], rs.at[i], dev)
        copy.start()
        copies.append(copy)
    return copies


def finish(copies):
    for copy in copies:
        copy.wait()


def gather_g(buf, ssy, rsy, ssc, rsc):
    _, _, c, y = place()
    sibling = {"context": 1 - c}
    own = c * NY + y
    copies, ahead = {}, []
    for dy in (2, 1, 3):
        copies[dy] = rcopy(
            buf.at[own], buf.at[own], ssy.at[dy - 1], rsy.at[dy - 1], {"dp": (y + dy) % NY}
        )
        copies[dy].start()
    cross = rcopy(buf.at[own], buf.at[own], ssc.at[0], rsc.at[0], sibling)
    cross.start()
    ahead.append(cross)
    for dy in (1, 3, 2):
        copies[dy].wait_recv()
        block = c * NY + (y + NY - dy) % NY
        cross = rcopy(buf.at[block], buf.at[block], ssc.at[dy], rsc.at[dy], sibling)
        cross.start()
        ahead.append(cross)
    for copy in ahead:
        copy.wait()
    for dy in (2, 1, 3):
        copies[dy].wait_send()


def reduce_tensor(part, bufs, compute_block, beside=None):
    ra, rb, sa, sb, ra2, rb2, s1, r1, s2, r2 = bufs
    x, z, _, _ = place()
    first, second = {}, {}
    for dx in X_ORDER + (0,):
        xb = (x + dx) % NX
        compute_block(xb)
        if dx:
            first["x", dx] = rcopy(
                part.at[xb, :, :, pl.ds(0, CA)],
                ra.at[x],
                s1.at[dx],
                r1.at[dx],
                {"tensor": xb * NZ + z},
            )
            first["x", dx].start()
    for dz in Z_ORDER:
        zb = (z + dz) % NZ
        first["z", dz] = rcopy(
            part.at[:, zb, :, pl.ds(CA, CB)],
            rb.at[z],
            s1.at[NX + dz],
            r1.at[NX + dz],
            {"tensor": x * NZ + zb},
        )
        first["z", dz].start()
    if beside is not None:
        beside()
    for dx in X_ORDER:
        first["x", dx].wait_recv()
    for dz in Z_ORDER + (0,):
        zb = (z + dz) % NZ
        total = part[x, zb, :, :CA]
        for dx in X_ORDER:
            total = total + ra[(x + NX - dx) % NX, zb]
        sa[zb] = total
        if dz:
            second["z", dz] = rcopy(
                sa.at[zb], ra2.at[z], s2.at[NX + dz], r2.at[NX + dz], {"tensor": x * NZ + zb}
            )
            second["z", dz].start()
    for dz in Z_ORDER:
        first["z", dz].wait_recv()
    for dx in X_ORDER + (0,):
        xb = (x + dx) % NX
        total = part[xb, z, :, CA:]
        for dz in Z_ORDER:
            total = total + rb[(z + NZ - dz) % NZ, xb]
        sb[xb] = total
        if dx:
            second["x", dx] = rcopy(
                sb.at[xb], rb2.at[x], s2.at[dx], r2.at[dx], {"tensor": xb * NZ + z}
            )
            second["x", dx].start()
    for copy in second.values():
        copy.wait_recv()
    left, right = sa[z], sb[x]
    for dz in Z_ORDER:
        left = left + ra2[(z + NZ - dz) % NZ]
    for dx in X_ORDER:
        right = right + rb2[(x + NX - dx) % NX]
    for copy in list(first.values()) + list(second.values()):
        copy.wait_send()
    return left, right


def reduce_scratch():
    return [
        pltpu.VMEM((NX, NZ, ROWS, CA), F32),
        pltpu.VMEM((NZ, NX, ROWS, CB), F32),
        pltpu.VMEM((NZ, ROWS, CA), F32),
        pltpu.VMEM((NX, ROWS, CB), F32),
        pltpu.VMEM((NZ, ROWS, CA), F32),
        pltpu.VMEM((NX, ROWS, CB), F32),
    ] + [pltpu.SemaphoreType.DMA((NX + NZ,))] * 4


def gather_tensor(buf, s1, r1, s2, r2):
    x, z, _, _ = place()
    left, right = pl.ds(0, CA), pl.ds(CA, CB)
    copies = {}

    def go(ref, ss, rs, name, slot, peer):
        copies[name] = rcopy(ref, ref, ss.at[slot], rs.at[slot], {"tensor": peer})
        copies[name].start()

    for dz in Z_ORDER:
        go(buf.at[x, z, :, left], s1, r1, (1, "z", dz), NX + dz, x * NZ + (z + dz) % NZ)
    for dx in X_ORDER:
        go(buf.at[x, z, :, right], s1, r1, (1, "x", dx), dx, (x + dx) % NX * NZ + z)
    for dx in X_ORDER:
        copies[1, "x", dx].wait_recv()
    for dz in Z_ORDER:
        go(buf.at[:, z, :, right], s2, r2, (2, "z", dz), NX + dz, x * NZ + (z + dz) % NZ)
    for dz in Z_ORDER:
        copies[1, "z", dz].wait_recv()
    for dx in X_ORDER:
        go(buf.at[x, :, :, left], s2, r2, (2, "x", dx), dx, (x + dx) % NX * NZ + z)
    for name, copy in copies.items():
        if name[0] == 2:
            copy.wait_recv()
    for copy in copies.values():
        copy.wait_send()


def rms(squares):
    return jnp.sqrt(squares / D + EPS)


def front_kernel(
    hidden_ref,
    ids_ref,
    gain_h_ref,
    gain_e_ref,
    gain_f_ref,
    table_ref,
    proj_h_ref,
    proj_e_ref,
    nh_ref,
    ne_ref,
    fn_ref,
    unit_ref,
    mrms_ref,
    hrms_ref,
    ids_all,
    ids_col,
    look,
    look_recv,
    stats,
    part,
    squares,
    ids_s,
    ids_r,
    emb_s,
    emb_r,
    st_s,
    st_r,
    gy_s,
    gy_r,
    gc_s,
    gc_r,
    sq_s,
    sq_r,
    ag_s1,
    ag_r1,
    ag_s2,
    ag_r2,
    *reduce_bufs,
):
    x, z, c, y = place()
    g = c * NY + y
    greet_all()
    ids_all[g] = ids_ref[...]
    sent_ids = share_g(ids_all, ids_s, ids_r)
    hidden = hidden_ref[...].astype(F32)
    hidden_squares = jnp.sum(hidden * hidden, axis=1, keepdims=True)
    finish(sent_ids)
    for b in range(NG):
        ids_col[pl.ds(b * OWN, OWN), :] = to_col(ids_all[b]) - g * TABLE

    step = 1024
    slab = 256

    def lookup(b, carry):
        column = ids_col[pl.ds(pl.multiple_of(b * slab, slab), slab), :]

        def chunk(k, total):
            hits = column == lax.broadcasted_iota(jnp.int32, (slab, step), 1) + k * step
            ones = jnp.where(hits, F32(1.0), F32(0.0)).astype(BF16)
            rows = table_ref[pl.ds(pl.multiple_of(k * step, step), step), :]
            return total + jnp.dot(ones, rows, preferred_element_type=F32)

        total = lax.fori_loop(0, TABLE // step, chunk, jnp.zeros((slab, FEAT), F32))
        look[pl.ds(b * 2, 2)] = total.astype(BF16).reshape(2, OWN, FEAT)
        return carry

    lax.fori_loop(0, NG * OWN // slab, lookup, 0)
    sent = scatter_g(look, look_recv, emb_s, emb_r)
    look_recv[g] = look[g]
    finish(sent)
    embedded = look_recv[0].astype(F32)
    for b in range(1, NG):
        embedded = embedded + look_recv[b].astype(F32)
    embed_squares = jnp.sum(embedded * embedded, axis=1, keepdims=True)
    tile = jnp.concatenate(
        [to_row(hidden_squares), to_row(embed_squares), jnp.zeros((6, OWN), F32)], axis=0
    )
    share_tensor(tile, stats, st_s, st_r)
    sums = jnp.sum(stats[...], axis=0)
    hidden_rms = rms(to_col(sums[:1, :]))
    embed_rms = rms(to_col(sums[1:2, :]))
    hrms_ref[...] = hidden_rms
    nh_ref[g] = (hidden / hidden_rms * gain_h_ref[...].astype(F32)).astype(BF16)
    ne_ref[g] = (embedded / embed_rms * gain_e_ref[...].astype(F32)).astype(BF16)
    gather_g(nh_ref, gy_s.at[0], gy_r.at[0], gc_s.at[0], gc_r.at[0])
    gather_g(ne_ref, gy_s.at[1], gy_r.at[1], gc_s.at[1], gc_r.at[1])

    def project(xb):
        nh = nh_ref[pl.ds(xb * 2, 2)].reshape(2 * OWN, FEAT)
        ne = ne_ref[pl.ds(xb * 2, 2)].reshape(2 * OWN, FEAT)
        terms = jnp.dot(nh, proj_h_ref[...], preferred_element_type=F32) + jnp.dot(
            ne, proj_e_ref[...], preferred_element_type=F32
        )
        part[xb] = terms.reshape(NZ, ROWS, WIDE)

    left, right = reduce_tensor(part, reduce_bufs, project)
    own_squares = jnp.sum(left * left, axis=1, keepdims=True) + jnp.sum(
        right * right, axis=1, keepdims=True
    )
    squares[g] = jnp.broadcast_to(own_squares, (ROWS, OWN))
    finish(share_g(squares, sq_s, sq_r))
    mixed_rms = rms(jnp.sum(squares[...], axis=0)[:, :1])
    mrms_ref[...] = mixed_rms
    left, right = left / mixed_rms, right / mixed_rms
    unit_ref[:, :CA] = left
    unit_ref[:, CA:] = right
    gain = gain_f_ref[...].astype(F32)
    fn_ref[x, z, :, :CA] = (left * gain[:, :CA]).astype(BF16)
    fn_ref[x, z, :, CA:] = (right * gain[:, CA:]).astype(BF16)
    gather_tensor(fn_ref, ag_s1, ag_r1, ag_s2, ag_r2)


def vmem(n):
    return [pl.BlockSpec(memory_space=pltpu.VMEM)] * n


def dma(*shape):
    return pltpu.SemaphoreType.DMA(shape)


def params(cid):
    return pltpu.CompilerParams(
        collective_id=cid, has_side_effects=True, vmem_limit_bytes=VMEM_LIMIT
    )


def front(hidden, ids, gain_h, gain_e, gain_f, table, proj_h, proj_e):
    return pl.pallas_call(
        front_kernel,
        out_shape=(
            jax.ShapeDtypeStruct((NG, OWN, FEAT), BF16),
            jax.ShapeDtypeStruct((NG, OWN, FEAT), BF16),
            jax.ShapeDtypeStruct((NX, NZ, ROWS, WIDE), BF16),
            jax.ShapeDtypeStruct((ROWS, WIDE), F32),
            jax.ShapeDtypeStruct((ROWS, 1), F32),
            jax.ShapeDtypeStruct((OWN, 1), F32),
        ),
        in_specs=vmem(8),
        out_specs=tuple(vmem(6)),
        scratch_shapes=[
            pltpu.VMEM((NG, 1, OWN), jnp.int32),
            pltpu.VMEM((NG * OWN, 1), jnp.int32),
            pltpu.VMEM((NG, OWN, FEAT), BF16),
            pltpu.VMEM((NG, OWN, FEAT), BF16),
            pltpu.VMEM((NT, 8, OWN), F32),
            pltpu.VMEM((NX, NZ, ROWS, WIDE), F32),
            pltpu.VMEM((NG, ROWS, OWN), F32),
            dma(NG - 1),
            dma(NG - 1),
            dma(NG - 1),
            dma(NG - 1),
            pltpu.SemaphoreType.DMA,
            pltpu.SemaphoreType.DMA,
            dma(2, 3),
            dma(2, 3),
            dma(2, 4),
            dma(2, 4),
            dma(NG - 1),
            dma(NG - 1),
        ]
        + [dma(NX + NZ)] * 4
        + reduce_scratch(),
        compiler_params=params(0),
        name="front",
    )(hidden, ids, gain_h, gain_e, gain_f, table, proj_h, proj_e)


CHUNKS = 4
CW = VOC // CHUNKS


def middle_kernel(
    fn_ref,
    head_ref,
    targets_ref,
    mask_ref,
    lg_ref,
    loss_ref,
    logits,
    core_recv,
    y_recv,
    stats,
    masks,
    losses,
    mk_s,
    mk_r,
    co_s,
    co_r,
    ry_s,
    ry_r,
    st_s,
    st_r,
    lo_s,
    lo_r,
    gy_s,
    gy_r,
    gc_s,
    gc_r,
):
    x, z, c, y = place()
    g = c * NY + y
    greet_all()
    mask = mask_ref[...].astype(F32)
    masks[g] = jnp.broadcast_to(mask, (8, OWN))
    sent_masks = share_g(masks, mk_s, mk_r)
    half = NY * OWN
    other = 1 - c

    def product(core, n):
        rows = fn_ref[pl.ds(core * 2, 2)].reshape(half, WIDE)
        terms = jnp.dot(
            rows, head_ref[:, n * CW : (n + 1) * CW], preferred_element_type=F32
        )
        logits[core, :, :, n * CW : (n + 1) * CW] = terms.reshape(NY, OWN, CW)

    crossing = []
    for n in range(CHUNKS):
        product(other, n)
        columns = pl.ds(n * CW, CW)
        copy = rcopy(
            logits.at[other, :, :, columns],
            core_recv.at[:, :, columns],
            co_s.at[n],
            co_r.at[n],
            {"context": other},
        )
        copy.start()
        crossing.append(copy)
    along = []
    for n in range(CHUNKS):
        product(c, n)
        columns = pl.ds(n * CW, CW)
        crossing[n].wait_recv()
        logits[c, :, :, columns] = logits[c, :, :, columns] + core_recv[:, :, columns]
        for dy in (2, 1, 3):
            yb = (y + dy) % NY
            copy = rcopy(
                logits.at[c, yb, :, columns],
                y_recv.at[dy - 1, :, columns],
                ry_s.at[n, dy - 1],
                ry_r.at[n, dy - 1],
                {"dp": yb},
            )
            copy.start()
            along.append(copy)
    target = to_col(targets_ref[...])
    finish(sent_masks)
    mask_total = jnp.sum(masks[...][:, :1, :])
    for copy in along:
        copy.wait_recv()
    for copy in along + crossing:
        copy.wait_send()
    own = logits[c, y] + y_recv[0] + y_recv[1] + y_recv[2]
    columns = lax.broadcasted_iota(jnp.int32, (1, VOC), 1) + (x * NZ + z) * VOC
    hits = columns == target
    top = jnp.max(own, axis=1, keepdims=True)
    total = jnp.sum(jnp.exp(own - top), axis=1, keepdims=True)
    picked = jnp.sum(jnp.where(hits, own, F32(0.0)), axis=1, keepdims=True)
    tile = jnp.concatenate(
        [to_row(top), to_row(total), to_row(picked), jnp.zeros((5, OWN), F32)], axis=0
    )
    share_tensor(tile, stats, st_s, st_r)
    every = stats[...]
    tops = every[:, 0, :]
    row_top = jnp.max(tops, axis=0, keepdims=True)
    exp_total = jnp.sum(every[:, 1, :] * jnp.exp(tops - row_top), axis=0, keepdims=True)
    picked = jnp.sum(every[:, 2, :], axis=0, keepdims=True)
    log_total = row_top + jnp.log(exp_total)
    losses[g] = jnp.broadcast_to(
        jnp.sum(mask * (log_total - picked), axis=1, keepdims=True), (8, OWN)
    )
    sent_losses = share_g(losses, lo_s, lo_r)
    probs = jnp.exp(own - to_col(log_total))
    weight = to_col(mask / mask_total)
    lg_ref[g] = (weight * (probs - jnp.where(hits, F32(1.0), F32(0.0)))).astype(BF16)
    gather_g(lg_ref, gy_s, gy_r, gc_s, gc_r)
    finish(sent_losses)
    loss_ref[...] = jnp.sum(losses[...], axis=0)[:1, :1] / mask_total


def middle(fn, head, targets, mask):
    return pl.pallas_call(
        middle_kernel,
        out_shape=(
            jax.ShapeDtypeStruct((NG, OWN, VOC), BF16),
            jax.ShapeDtypeStruct((1, 1), F32),
        ),
        in_specs=vmem(4),
        out_specs=tuple(vmem(2)),
        scratch_shapes=[
            pltpu.VMEM((NC, NY, OWN, VOC), F32),
            pltpu.VMEM((NY, OWN, VOC), F32),
            pltpu.VMEM((NY - 1, OWN, VOC), F32),
            pltpu.VMEM((NT, 8, OWN), F32),
            pltpu.VMEM((NG, 8, OWN), F32),
            pltpu.VMEM((NG, 8, OWN), F32),
            dma(NG - 1),
            dma(NG - 1),
            dma(CHUNKS),
            dma(CHUNKS),
            dma(CHUNKS, 3),
            dma(CHUNKS, 3),
            pltpu.SemaphoreType.DMA,
            pltpu.SemaphoreType.DMA,
            dma(NG - 1),
            dma(NG - 1),
            dma(3),
            dma(3),
            dma(4),
            dma(4),
        ],
        compiler_params=params(1),
        name="middle",
    )(fn, head, targets, mask)


def back_kernel(
    lg_ref,
    fn_ref,
    head_ref,
    unit_ref,
    mrms_ref,
    gain_f_ref,
    nh_ref,
    ne_ref,
    proj_h_ref,
    hidden_ref,
    hrms_ref,
    gain_h_ref,
    hidden_grad_ref,
    ph_grad_ref,
    pe_grad_ref,
    head_grad_ref,
    part,
    flipped,
    inners,
    mg,
    nhg,
    nhg_recv,
    stats,
    in_s,
    in_r,
    ng_s,
    ng_r,
    st_s,
    st_r,
    ag_s1,
    ag_r1,
    ag_s2,
    ag_r2,
    *reduce_bufs,
):
    x, z, c, y = place()
    g = c * NY + y
    greet_all()

    def terms(xb):
        rows = lg_ref[pl.ds(xb * 2, 2)].reshape(2 * OWN, VOC)
        out = lax.dot_general(
            rows, head_ref[...], (((1,), (1,)), ((), ())), preferred_element_type=F32
        )
        part[xb] = out.reshape(NZ, ROWS, WIDE)

    def head_side():
        for xb in range(NX):
            flipped[:, xb * 256 : (xb + 1) * 256] = fn_ref[xb].reshape(256, WIDE).T

        def tile(n, carry):
            columns = pl.ds(pl.multiple_of(n * 256, 256), 256)
            grads = lg_ref[:, :, columns].reshape(NG * OWN, 256)
            head_grad_ref[:, columns] = jnp.dot(
                flipped[...], grads, preferred_element_type=F32
            ).astype(BF16)
            return carry

        lax.fori_loop(0, VOC // 256, tile, 0)

    left, right = reduce_tensor(part, reduce_bufs, terms, head_side)
    gain = gain_f_ref[...].astype(F32)
    left, right = left * gain[:, :CA], right * gain[:, CA:]
    unit = unit_ref[...]
    own_inner = jnp.sum(left * unit[:, :CA], axis=1, keepdims=True) + jnp.sum(
        right * unit[:, CA:], axis=1, keepdims=True
    )
    inners[g] = jnp.broadcast_to(own_inner, (ROWS, OWN))
    finish(share_g(inners, in_s, in_r))
    inner = jnp.sum(inners[...], axis=0)[:, :1] / D
    mixed_rms = mrms_ref[...]
    mg[x, z, :, :CA] = ((left - unit[:, :CA] * inner) / mixed_rms).astype(BF16)
    mg[x, z, :, CA:] = ((right - unit[:, CA:] * inner) / mixed_rms).astype(BF16)
    gather_tensor(mg, ag_s1, ag_r1, ag_s2, ag_r2)
    grads = mg[...].reshape(NG * OWN, WIDE)
    nhg[...] = lax.dot_general(
        grads, proj_h_ref[...], (((1,), (1,)), ((), ())), preferred_element_type=F32
    ).reshape(NG, OWN, FEAT)
    sent = scatter_g(nhg, nhg_recv, ng_s, ng_r)
    nhg_recv[g] = nhg[g]
    over_rows = (((0,), (0,)), ((), ()))
    ph_grad_ref[...] = lax.dot_general(
        nh_ref[...].reshape(NG * OWN, FEAT), grads, over_rows, preferred_element_type=F32
    ).astype(BF16)
    pe_grad_ref[...] = lax.dot_general(
        ne_ref[...].reshape(NG * OWN, FEAT), grads, over_rows, preferred_element_type=F32
    ).astype(BF16)
    finish(sent)
    scaled = jnp.sum(nhg_recv[...], axis=0) * gain_h_ref[...].astype(F32)
    hidden_rms = hrms_ref[...]
    hidden_unit = hidden_ref[...].astype(F32) / hidden_rms
    inner = jnp.sum(scaled * hidden_unit, axis=1, keepdims=True)
    tile = jnp.broadcast_to(to_row(inner), (8, OWN))
    share_tensor(tile, stats, st_s, st_r)
    inner = to_col(jnp.sum(stats[...], axis=0)[:1, :]) / D
    hidden_grad_ref[...] = ((scaled - hidden_unit * inner) / hidden_rms).astype(BF16)


def back(*args):
    return pl.pallas_call(
        back_kernel,
        out_shape=(
            jax.ShapeDtypeStruct((OWN, FEAT), BF16),
            jax.ShapeDtypeStruct((FEAT, WIDE), BF16),
            jax.ShapeDtypeStruct((FEAT, WIDE), BF16),
            jax.ShapeDtypeStruct((WIDE, VOC), BF16),
        ),
        in_specs=vmem(12),
        out_specs=tuple(vmem(4)),
        scratch_shapes=[
            pltpu.VMEM((NX, NZ, ROWS, WIDE), F32),
            pltpu.VMEM((WIDE, NG * OWN), BF16),
            pltpu.VMEM((NG, ROWS, OWN), F32),
            pltpu.VMEM((NX, NZ, ROWS, WIDE), BF16),
            pltpu.VMEM((NG, OWN, FEAT), F32),
            pltpu.VMEM((NG, OWN, FEAT), F32),
            pltpu.VMEM((NT, 8, OWN), F32),
            dma(NG - 1),
            dma(NG - 1),
            dma(NG - 1),
            dma(NG - 1),
            pltpu.SemaphoreType.DMA,
            pltpu.SemaphoreType.DMA,
        ]
        + [dma(NX + NZ)] * 4
        + reduce_scratch(),
        compiler_params=params(2),
        name="back",
    )(*args)


def per_device(
    hidden_prev,
    next_ids,
    targets,
    loss_mask,
    gain_hidden,
    gain_embed,
    gain_final,
    embed_table,
    proj_hidden,
    proj_embed,
    head_weight,
):
    gain_h, gain_e, gain_f = gain_hidden[None, :], gain_embed[None, :], gain_final[None, :]
    nh, ne, fn, unit, mixed_rms, hidden_rms = front(
        hidden_prev, next_ids[None, :], gain_h, gain_e, gain_f, embed_table, proj_hidden, proj_embed
    )
    lg, loss = middle(fn, head_weight, targets[None, :], loss_mask[None, :])
    hidden_grad, ph_grad, pe_grad, head_grad = back(
        lg,
        fn,
        head_weight,
        unit,
        mixed_rms,
        gain_f,
        nh,
        ne,
        proj_hidden,
        hidden_prev,
        hidden_rms,
        gain_h,
    )
    return (loss[0, 0], hidden_grad, ph_grad, pe_grad, head_grad)


def solution(mesh):
    return jax.shard_map(
        per_device,
        mesh=mesh,
        in_specs=(
            P(("context", "dp"), "tensor"),
            P(("context", "dp")),
            P(("context", "dp")),
            P(("context", "dp")),
            P("tensor"),
            P("tensor"),
            P(("context", "dp")),
            P(("context", "dp"), "tensor"),
            P("tensor", ("context", "dp")),
            P("tensor", ("context", "dp")),
            P(("context", "dp"), "tensor"),
        ),
        out_specs=(
            P(),
            P(("context", "dp"), "tensor"),
            P("tensor", ("context", "dp")),
            P("tensor", ("context", "dp")),
            P(("context", "dp"), "tensor"),
        ),
        check_vma=False,
    )
```

time: 984 us -> 368 us (0.37); the launches traced: 972 us -> 367 us
  waiting for transfers between devices: 508 us -> 0 us
  blocking collectives: 373 us -> 0 us
  Pallas kernels: 0 us -> 344 us
  matrix products: 39.1 us -> 0 us
  other arithmetic: 21.6 us -> 0 us
  between operations: 16.8 us -> 2.36 us
    psum x3 -> x0, waiting for transfers between devices: 371 us -> none  [the longest x1 157 us: per_device(): final_grad = lax.psum(final_terms, 'tensor')]
    pallas_call x0 -> x3, Pallas kernels: none -> 344 us  [the longest x1 136 us: front(): pl.pallas_call(front_kernel, out_shape=(jax.ShapeDtypeStruct((NG, OWN, FE...]
    psum x6 -> x0, blocking collectives: 258 us -> none  [the longest x1 62 us: per_device(): embed_total = lax.psum(jnp.sum(embedded * embedded, axis=1), 'tensor')]
    reduce_scatter x2 -> x0, waiting for transfers between devices: 108 us -> none  [the longest x1 89.7 us: per_device(): lax.psum_scatter(jnp.dot(final_normed, head_weight, preferred_element_typ...]
    pmax x1 -> x0, blocking collectives: 61 us -> none  [per_device(): row_top = lax.pmax(local_top, 'tensor')]
    all_gather x2 -> x0, blocking collectives: 54.2 us -> none  [the longest x1 38.3 us: per_device(): lax.all_gather(own_hidden, ('context', 'dp'), axis=0, tiled=True)]
    dot_general x8 -> x0, matrix products: 39.1 us -> none  [the longest x1 10.9 us: per_device(): jnp.dot(final_normed, head_weight, preferred_element_type=jnp.float32)]
    all_gather x1 -> x0, waiting for transfers between devices: 28.6 us -> none  [per_device(): lax.all_gather(logit_grad, ('context', 'dp'), axis=0, tiled=True)]
  transfers between devices with their start and end apart: 6 -> 0, of which waited for: 6 -> 0; matrix products, arithmetic and copies ran while one was open for 1% -> 0% of each run, Pallas kernels for 0% -> 0%
where the time goes in v1:
time: 368 us; the launch traced here: 367 us
  Pallas kernels  344 us (93%)
  local copies, waits for them, and re-layouts  21 us (6%)
    pallas_call x1, Pallas kernels, front(): pl.pallas_call(front_kernel, out_shape=(jax.ShapeDtypeStruct((NG, OWN, FE...  136 us
    pallas_call x1, Pallas kernels, back(): pl.pallas_call(back_kernel, out_shape=(jax.ShapeDtypeStruct((OWN, FEAT),...  111 us
    pallas_call x1, Pallas kernels, middle(): pl.pallas_call(middle_kernel, out_shape=(jax.ShapeDtypeStruct((NG, OWN, V...  96.5 us
    unnamed x6, local copies, waits for them, and re-layouts  17.3 us

profile of v1, /device:TPU:1, one launch (start us, length us, event | category | flops | bytes accessed | tf_op | source)
XLA Modules:
  0.0 367.2 jit_solution(11468276692487192034)
XLA Ops:
  0.6 1.2 broadcast_in_dim.19.gain_h_ref
  1.9 1.2 broadcast_in_dim.20.gain_e_ref
  3.1 1.3 broadcast_in_dim.21.gain_f_ref
  4.3 1.6 copy.16.hidden_ref
  5.9 6.3 %copy.17.table_ref = bf16[8192,224]{1,0:T(8,128)(2,1)} copy(bf16[8192,224]{0,1:T(8,128)(2,1)} %param.18) | data formatting | bytes 7340032 | tf_op args[7]
  12.1 136.5 %front.1 = (bf16[8,128,224]{2,1,0:T(8,128)(2,1)}, bf16[8,128,224]{2,1,0:T(8,128)(2,1)}, bf16[4,8,32,896]{3,2,1,0:T(8,128)(2,1)}, f32[32,896]{1,0:T(8,128)}, f32[32,1]{1,0:T(8,128)}, /*index=5*/f32[128,1]{1,0:T(8,128)}) custom-call(bf16[128,224]{1,0:T(8,128)(2,1)} %copy.16.hidden_ref, s32[1,128]{1,0:T(1,128)} %bitcast.6, ...), custom_call_target="tpu_custom_call" | custom-call | tf_op jit(solution)/shard_map/front/pallas_call | solution.py:387
  148.6 96.5 %middle.1 = (bf16[8,128,2048]{2,1,0:T(8,128)(2,1)}, f32[1,1]{1,0:T(1,128)}) custom-call(bf16[4,8,32,896]{3,2,1,0:T(8,128)(2,1)} %get-tuple-element.17.fn_ref, bf16[896,2048]{1,0:T(8,128)(2,1)} %head_ref.3, s32[1,128]{1,0:T(1,128)} %bitcast.4, s32[1,128]{1,0:T(1,128)} %bitcast.5), custom_call_target="tpu_custom_call" | custom-call | tf_op jit(solution)/shard_map/middle/pallas_call | solution.py:541
  245.1 110.9 %back.1 = (bf16[128,224]{1,0:T(8,128)(2,1)}, bf16[224,896]{1,0:T(8,128)(2,1)}, bf16[224,896]{1,0:T(8,128)(2,1)}, bf16[896,2048]{1,0:T(8,128)(2,1)}) custom-call(bf16[8,128,2048]{2,1,0:T(8,128)(2,1)} %get-tuple-element.19.lg_ref, bf16[4,8,32,896]{3,2,1,0:T(8,128)(2,1)} %get-tuple-element.17.fn_ref, bf16[896,2048]{1,0:T(8,128)(2,1)} %head_ref.3, ...), custom_call_target="tpu_custom_call" | custom-call | tf_op jit(solution)/shard_map/back/pallas_call | solution.py:676
  356.0 1.6 copy.19
  358.1 1.8 copy.25
  359.9 1.8 copy.26
  361.7 4.4 %copy.27 = bf16[896,2048]{1,0:T(8,128)(2,1)} copy(bf16[896,2048]{1,0:T(8,128)(2,1)} %get-tuple-element.43) | data formatting | bytes 7340032

commit v2 on v0

v2 whole, which is shorter than its diff:
```python
from typing import NamedTuple

import jax
import jax.numpy as jnp
from jax import lax
from jax.experimental import pallas as pl
from jax.experimental.pallas import tpu as pltpu
from jax.sharding import PartitionSpec as P

D = 7168
EPS = 1e-06
MESH = pl.DeviceIdType.MESH
F32 = jnp.float32
BF16 = jnp.bfloat16
NX, NZ, NC, NY = 4, 8, 2, 4
NT, NG = NX * NZ, NC * NY
ROWS = 32
OWN = 128
WIDE = 896
FEAT = 224
VOC = 2048
TABLE = 8192
Z_ORDER = (4, 3, 5, 2, 6, 1, 7)
VMEM_LIMIT = 62 * 1024 * 1024
PARTS = 2
R = ROWS // PARTS
TOK = NX * NZ * R
GR = OWN // PARTS
CHUNKS = 2
CW = VOC // CHUNKS


def place():
    t = lax.axis_index("tensor")
    return t // NZ, t % NZ, lax.axis_index("context"), lax.axis_index("dp")


def rcopy(src, dst, ss, rs, dev):
    return pltpu.make_async_remote_copy(
        src_ref=src, dst_ref=dst, send_sem=ss, recv_sem=rs, device_id=dev, device_id_type=MESH
    )


def greet_all():
    x, z, c, y = place()
    t = x * NZ + z
    bar = pltpu.get_barrier_semaphore()

    def hello(k, carry):
        pl.semaphore_signal(
            bar, inc=1, device_id={"tensor": (t + k) % NT}, device_id_type=MESH
        )
        return carry

    lax.fori_loop(1, NT, hello, 0)
    for dc in range(NC):
        for dy in range(NY):
            if dc or dy:
                pl.semaphore_signal(
                    bar,
                    inc=1,
                    device_id={"context": (c + dc) % NC, "dp": (y + dy) % NY},
                    device_id_type=MESH,
                )
    return bar


def to_tile(columns):
    n = columns[0].shape[0]
    lane = lax.broadcasted_iota(jnp.int32, (n, OWN), 1)
    wide = jnp.zeros((n, OWN), F32)
    for i, column in enumerate(columns):
        wide = jnp.where(lane == i, column, wide)
    if n < OWN:
        wide = jnp.concatenate([wide] * (OWN // n), axis=0)
    return wide.T[:8, :]


def to_col(row, n=OWN):
    return jnp.broadcast_to(row, (OWN, OWN)).T[:n, :1]


def share_tensor(tile, recv, ss, rs):
    x, z, _, _ = place()
    t = x * NZ + z
    recv[t] = tile

    def send(k, carry):
        rcopy(recv.at[t], recv.at[t], ss, rs, {"tensor": (t + k) % NT}).start()
        return carry

    lax.fori_loop(1, NT, send, 0)
    return [
        rcopy(
            recv.at[pl.ds(0, NT - 1)], recv.at[pl.ds(0, NT - 1)], ss, rs, {"tensor": (t + 1) % NT}
        )
    ]


def g_peers():
    _, _, c, y = place()
    for dy in (2, 1, 3, 0):
        for dc in (1, 0):
            if dc or dy:
                cb, yb = (c + dc) % NC, (y + dy) % NY
                yield cb * NY + yb, {"context": cb, "dp": yb}


def share_g(recv, ss, rs):
    _, _, c, y = place()
    g = c * NY + y
    copies = []
    for i, (_, dev) in enumerate(g_peers()):
        copy = rcopy(recv.at[g], recv.at[g], ss.at[i], rs.at[i], dev)
        copy.start()
        copies.append(copy)
    return copies


def scatter_g(src, recv, ss, rs):
    _, _, c, y = place()
    g = c * NY + y
    copies = []
    for i, (gb, dev) in enumerate(g_peers()):
        copy = rcopy(src.at[gb], recv.at[g], ss.at[i], rs.at[i], dev)
        copy.start()
        copies.append(copy)
    return copies


def arrive(copies):
    for copy in copies:
        copy.wait_recv()


def finish(copies):
    for copy in copies:
        copy.wait()


def g_block(ref, g):
    return ref.at[g // 2, pl.ds(g % 2 * 4, 4)]


def gather_g(buf, ssy, rsy, ssc, rsc, done):
    _, _, c, y = place()
    own, near = (c * NY + (y + dy) % NY for dy in (0, 1))
    before, far = (c * NY + (y + dy) % NY for dy in (3, 2))
    copies, ahead = [], []

    def go(ref, i, dev):
        copies.append(rcopy(ref, ref, ssy.at[i], rsy.at[i], dev))
        copies[-1].start()

    def cross(block, i):
        ref = g_block(buf, block)
        ahead.append(rcopy(ref, ref, ssc.at[i], rsc.at[i], {"context": 1 - c}))
        ahead[-1].start()

    up, down = {"dp": (y + 1) % NY}, {"dp": (y + 3) % NY}
    go(g_block(buf, own), 0, up)
    go(g_block(buf, own), 1, down)
    cross(own, 0)
    yield
    copies[0].wait_recv()
    go(g_block(buf, before).at[pl.ds(0, 2)], 2, up)
    cross(before, 1)
    copies[1].wait_recv()
    go(g_block(buf, near).at[pl.ds(2, 2)], 3, down)
    cross(near, 2)
    yield
    copies[2].wait_recv()
    copies[3].wait_recv()
    cross(far, 3)
    yield
    arrive(ahead)
    done += ahead + copies


def reduce_tensor(part, bufs, compute_block, done, result):
    first, near, line, last, s1, r1, s2, r2 = bufs
    x, z, _, _ = place()
    low, high = pl.ds(0, NZ // 2), pl.ds(NZ // 2, NZ // 2)
    after, far, before = ((x + dx) % NX for dx in (1, 2, 3))
    up, down = {"tensor": after * NZ + z}, {"tensor": before * NZ + z}
    copies = []

    def go(src, dst, i, dev):
        copies.append(rcopy(src, dst, s1.at[i], r1.at[i], dev))
        copies[-1].start()

    compute_block(far)
    go(part.at[far, low], first.at[0], 0, up)
    go(part.at[far, high], first.at[1], 1, down)
    compute_block(after)
    go(part.at[after, high], near.at[0, high], 2, up)
    compute_block(before)
    go(part.at[before, low], near.at[1, low], 3, down)
    compute_block(x)
    yield
    copies[0].wait_recv()
    part[after, low] = part[after, low] + first[0]
    go(part.at[after, low], near.at[0, low], 4, up)
    copies[1].wait_recv()
    part[before, high] = part[before, high] + first[1]
    go(part.at[before, high], near.at[1, high], 5, down)
    yield
    arrive(copies[2:])
    second = []
    for dz in Z_ORDER + (0,):
        zb = (z + dz) % NZ
        line[zb] = part[x, zb] + near[0, zb] + near[1, zb]
        if dz:
            second.append(
                rcopy(line.at[zb], last.at[z], s2.at[dz], r2.at[dz], {"tensor": x * NZ + zb})
            )
            second[-1].start()
    yield
    arrive(second)
    total = line[z]
    for dz in Z_ORDER:
        total = total + last[(z + NZ - dz) % NZ]
    for copy in copies + second:
        copy.wait_send()
    result.append(total)


def reduce_scratch():
    return [
        pltpu.VMEM((PARTS, NX, NZ, R, WIDE), F32),
        pltpu.VMEM((PARTS, 2, NZ // 2, R, WIDE), F32),
        pltpu.VMEM((PARTS, 2, NZ, R, WIDE), F32),
        pltpu.VMEM((PARTS, NZ, R, WIDE), F32),
        pltpu.VMEM((PARTS, NZ, R, WIDE), F32),
    ]


def gather_tensor(buf, s1, r1, s2, r2, done):
    x, z, _, _ = place()
    low, high = pl.ds(0, NZ // 2), pl.ds(NZ // 2, NZ // 2)
    after, before = (x + 1) % NX, (x + 3) % NX
    up, down = {"tensor": after * NZ + z}, {"tensor": before * NZ + z}
    first, second = [], []
    for dz in Z_ORDER:
        ref = buf.at[x, z]
        first.append(
            rcopy(ref, ref, s1.at[dz], r1.at[dz], {"tensor": x * NZ + (z + dz) % NZ})
        )
        first[-1].start()

    def go(ref, i, dev):
        second.append(rcopy(ref, ref, s2.at[i], r2.at[i], dev))
        second[-1].start()

    yield
    arrive(first)
    go(buf.at[x, low], 0, up)
    go(buf.at[x, high], 1, down)
    go(buf.at[x, high], 2, up)
    go(buf.at[x, low], 3, down)
    yield
    second[0].wait_recv()
    go(buf.at[before, low], 4, up)
    second[1].wait_recv()
    go(buf.at[after, high], 5, down)
    yield
    arrive(second[2:])
    done += first + second


def rms(squares):
    return jnp.sqrt(squares / D + EPS)


class Refs(NamedTuple):
    hidden: object
    ids: object
    targets: object
    mask: object
    gain_h: object
    gain_e: object
    gain_f: object
    table_in: object
    proj_h_in: object
    proj_e_in: object
    head_in: object
    loss: object
    hidden_grad: object
    ph_grad: object
    pe_grad: object
    head_grad: object
    table: object
    proj_h: object
    proj_e: object
    head: object
    load_sems: object
    rms_all: object
    ids_all: object
    ids_col: object
    look: object
    look_recv: object
    nh: object
    ne: object
    unit: object
    fn: object
    logits: object
    core_recv: object
    y_recv: object
    lg: object
    flipped: object
    mg: object
    nhg: object
    nhg_recv: object
    sums: object
    part: object
    first: object
    near: object
    line: object
    last: object
    hidden_stats: object
    front_stats: object
    soft_stats: object
    last_stats: object
    masks: object
    losses: object
    squares: object
    inners: object
    ids_s: object
    ids_r: object
    emb_s: object
    emb_r: object
    hst_s: object
    hst_r: object
    fst_s: object
    fst_r: object
    rm_s: object
    rm_r: object
    gy_s: object
    gy_r: object
    gc_s: object
    gc_r: object
    mk_s: object
    mk_r: object
    red_s1: object
    red_r1: object
    red_s2: object
    red_r2: object
    sq_s: object
    sq_r: object
    agt_s1: object
    agt_r1: object
    agt_s2: object
    agt_r2: object
    co_s: object
    co_r: object
    ry_s: object
    ry_r: object
    st_s: object
    st_r: object
    lo_s: object
    lo_r: object
    ly_s: object
    ly_r: object
    lc_s: object
    lc_r: object
    ng_s: object
    ng_r: object
    ls_s: object
    ls_r: object


def kernel(*refs):
    k = Refs(*refs)
    x, z, c, y = place()
    t = x * NZ + z
    g = c * NY + y
    bar = greet_all()
    done = []
    loads = [
        pltpu.make_async_copy(src, dst, k.load_sems.at[i])
        for i, (src, dst) in enumerate(
            (
                (k.table_in, k.table),
                (k.proj_h_in, k.proj_h),
                (k.proj_e_in, k.proj_e),
                (k.head_in, k.head),
            )
        )
    ]
    for load in loads:
        load.start()
    hidden = k.hidden[...].astype(F32).T
    hidden_squares = jnp.sum(hidden * hidden, axis=1, keepdims=True)
    hidden_tile = to_tile([hidden_squares])
    pl.semaphore_wait(bar, NT - 1 + NG - 1)

    k.ids_all[g] = k.ids[...]
    sent_ids = share_g(k.ids_all, k.ids_s, k.ids_r)
    mask = k.mask[...].astype(F32)
    k.masks[g] = jnp.broadcast_to(mask, (8, OWN))
    sent_masks = share_g(k.masks, k.mk_s, k.mk_r)
    hidden_sent = share_tensor(hidden_tile, k.hidden_stats, k.hst_s, k.hst_r)
    arrive(sent_ids)
    done += sent_ids
    for b in range(NG):
        k.ids_col[pl.ds(b * OWN, OWN), :] = to_col(k.ids_all[b]) - g * TABLE

    loads[0].wait()
    step = 512

    def lookup(j, total):
        hits = k.ids_col[...] == lax.broadcasted_iota(jnp.int32, (1, step), 1) + j * step
        ones = jnp.where(hits, F32(1.0), F32(0.0)).astype(BF16)
        rows = k.table[:, pl.ds(pl.multiple_of(j * step, step), step)]
        return total + lax.dot_general(
            ones, rows, (((1,), (1,)), ((), ())), preferred_element_type=F32
        )

    total = lax.fori_loop(0, TABLE // step, lookup, jnp.zeros((NG * OWN, FEAT), F32))
    k.look[...] = total.astype(BF16).reshape(NG, OWN, FEAT)
    sent = scatter_g(k.look, k.look_recv, k.emb_s, k.emb_r)
    finish(hidden_sent)
    hidden_rms = rms(to_col(jnp.sum(k.hidden_stats[...], axis=0)[:1, :]))
    hidden_unit = hidden / hidden_rms
    k.sums[:, :FEAT] = hidden_unit
    k.sums[:, FEAT : FEAT + 1] = hidden_rms
    gain_h = k.gain_h[...].astype(F32)[None, :]
    gain_f = k.gain_f[...].astype(F32)[None, :]
    nh = (hidden_unit * gain_h).astype(BF16)
    k.nh[g // 2, pl.ds(g % 2 * 4, 4)] = nh.reshape(4, ROWS, FEAT)
    gather_nh = gather_g(k.nh, k.gy_s.at[0], k.gy_r.at[0], k.gc_s.at[0], k.gc_r.at[0], done)
    next(gather_nh)
    k.look_recv[g] = k.look[g]
    arrive(sent)
    done += sent
    embedded = k.look_recv[0].astype(F32)
    for b in range(1, NG):
        embedded = embedded + k.look_recv[b].astype(F32)
    embed_squares = jnp.sum(embedded * embedded, axis=1, keepdims=True)
    sent = share_tensor(to_tile([embed_squares]), k.front_stats, k.fst_s, k.fst_r)
    k.ne[g // 2, pl.ds(g % 2 * 4, 4)] = embedded.astype(BF16).reshape(4, ROWS, FEAT)
    gather_ne = gather_g(k.ne, k.gy_s.at[1], k.gy_r.at[1], k.gc_s.at[1], k.gc_r.at[1], done)
    next(gather_ne)
    next(gather_nh)
    finish(sent)
    embed_rms = rms(jnp.sum(k.front_stats[...], axis=0))
    k.rms_all[g] = embed_rms
    sent = share_g(k.rms_all, k.rm_s, k.rm_r)
    for one in (gather_ne, gather_nh, gather_ne, gather_nh, gather_ne):
        next(one, None)
    arrive(sent)
    done += sent
    gain_e = k.gain_e[...].astype(F32)[None, :]
    for one in done:
        one.wait_send()
    done = []
    for b in range(NG):
        raw = k.ne[b // 2, pl.ds(b % 2 * 4, 4)].reshape(OWN, FEAT).astype(F32)
        ne = (raw / to_col(k.rms_all[b][:1, :]) * gain_e).astype(BF16)
        k.ne[b // 2, pl.ds(b % 2 * 4, 4)] = ne.reshape(4, ROWS, FEAT)
    loads[1].wait()
    loads[2].wait()
    arrive(sent_masks)
    done += sent_masks
    mask_total = jnp.sum(k.masks[...][:, :1, :])
    weight = to_col(mask / mask_total)
    target = to_col(k.targets[...])
    mask = to_col(mask)

    def own_rows(array, p):
        return array.reshape(4, ROWS, array.shape[1])[:, p * R : (p + 1) * R].reshape(
            GR, array.shape[1]
        )

    def chain(p):
        bufs = [ref.at[p] for ref in (k.first, k.near, k.line, k.last)]
        part, fn, lg, mg = k.part.at[p], k.fn.at[p], k.lg.at[p], k.mg.at[p]
        logits, core_recv, y_recv = k.logits.at[p], k.core_recv.at[p], k.y_recv.at[p]
        rows = slice(p * R, (p + 1) * R)

        def sems(i):
            return [ref.at[p, i] for ref in (k.red_s1, k.red_r1, k.red_s2, k.red_r2)]

        def agt(i):
            return [ref.at[p, i] for ref in (k.agt_s1, k.agt_r1, k.agt_s2, k.agt_r2)]

        def project(xb):
            nh = k.nh[xb, :, rows, :].reshape(NZ * R, FEAT)
            ne = k.ne[xb, :, rows, :].reshape(NZ * R, FEAT)
            terms = jnp.dot(nh, k.proj_h[...], preferred_element_type=F32) + jnp.dot(
                ne, k.proj_e[...], preferred_element_type=F32
            )
            part[xb] = terms.reshape(NZ, R, WIDE)

        mixed = []
        steps = reduce_tensor(part, bufs + sems(0), project, done, mixed)
        next(steps)
        yield "rs1a"
        next(steps)
        yield "rs1x"
        next(steps)
        yield "rs1b"
        next(steps, None)
        mixed = mixed[0]
        own_squares = jnp.sum(mixed * mixed, axis=1, keepdims=True)
        k.squares[p, g] = jnp.broadcast_to(own_squares, (R, OWN))
        sent = share_g(k.squares.at[p], k.sq_s.at[p], k.sq_r.at[p])
        yield "sq"
        finish(sent)
        mixed_rms = rms(jnp.sum(k.squares[p], axis=0)[:, :1])
        mixed = mixed / mixed_rms
        k.unit[p] = mixed
        fn[x, z] = (mixed * gain_f).astype(BF16)
        steps = gather_tensor(fn, *agt(0), done)
        next(steps)
        yield "ag1"
        next(steps)
        yield "ag2"
        next(steps)
        yield "agx"
        next(steps, None)
        if p == 0:
            loads[3].wait()
        half = NY * GR
        other = 1 - c

        def product(core, n):
            out = jnp.dot(
                fn[pl.ds(core * 2, 2)].reshape(half, WIDE),
                k.head[:, n * CW : (n + 1) * CW],
                preferred_element_type=F32,
            )
            logits[core, :, :, n * CW : (n + 1) * CW] = out.reshape(NY, GR, CW)

        crossing, along = [], []
        for n in range(CHUNKS):
            product(other, n)
            columns = pl.ds(n * CW, CW)
            copy = rcopy(
                logits.at[other, :, :, columns],
                core_recv.at[:, :, columns],
                k.co_s.at[p, n],
                k.co_r.at[p, n],
                {"context": other},
            )
            copy.start()
            crossing.append(copy)
        after, far, before = ((y + dy) % NY for dy in (1, 2, 3))
        up, down = {"dp": after}, {"dp": before}

        def along_y(src, dst, i, dev):
            along.append(rcopy(src, dst, k.ry_s.at[p, i], k.ry_r.at[p, i], dev))
            along[-1].start()

        low, high = pl.ds(0, CW), pl.ds(CW, CW)
        for n, columns in enumerate((low, high)):
            product(c, n)
            crossing[n].wait_recv()
            logits[c, :, :, columns] = logits[c, :, :, columns] + core_recv[:, :, columns]
            far_to, near_to, slot, near = ((up, down, 1, before), (down, up, 0, after))[n]
            along_y(logits.at[c, far, :, columns], y_recv.at[2, :, columns], 2 * n, far_to)
            along_y(
                logits.at[c, near, :, columns], y_recv.at[slot, :, columns], 2 * n + 1, near_to
            )
        flipped = k.flipped.at[p]
        for xb in range(NX):
            block = NZ * R
            flipped[:, xb * block : (xb + 1) * block] = fn[xb].reshape(block, WIDE).T
        yield "ry"
        along[0].wait_recv()
        logits[c, after, :, low] = logits[c, after, :, low] + y_recv[2, :, low]
        along_y(logits.at[c, after, :, low], y_recv.at[0, :, low], 4, up)
        along[2].wait_recv()
        logits[c, before, :, high] = logits[c, before, :, high] + y_recv[2, :, high]
        along_y(logits.at[c, before, :, high], y_recv.at[1, :, high], 5, down)
        yield "ryx"
        arrive([along[1], along[3], along[4], along[5]])
        done.extend(along + crossing)
        own = logits[c, y] + y_recv[0] + y_recv[1]
        logits[c, y] = own
        columns = lax.broadcasted_iota(jnp.int32, (1, VOC), 1) + t * VOC
        hits = columns == own_rows(target, p)
        top = jnp.max(own, axis=1, keepdims=True)
        total = jnp.sum(jnp.exp(own - top), axis=1, keepdims=True)
        picked = jnp.sum(jnp.where(hits, own, F32(0.0)), axis=1, keepdims=True)
        sent = share_tensor(
            to_tile([top, total, picked]), k.soft_stats.at[p], k.st_s.at[p], k.st_r.at[p]
        )
        yield "st"
        finish(sent)
        every = k.soft_stats[p]
        tops = every[:, 0, :]
        row_top = jnp.max(tops, axis=0, keepdims=True)
        exp_total = jnp.sum(every[:, 1, :] * jnp.exp(tops - row_top), axis=0, keepdims=True)
        picked = to_col(jnp.sum(every[:, 2, :], axis=0, keepdims=True), GR)
        log_total = to_col(row_top + jnp.log(exp_total), GR)
        own = logits[c, y]
        probs = jnp.exp(own - log_total)
        grads = own_rows(weight, p) * (probs - jnp.where(hits, F32(1.0), F32(0.0)))
        lg[g // 2, pl.ds(g % 2 * 4, 4)] = grads.astype(BF16).reshape(4, R, VOC)
        steps = gather_g(lg, k.ly_s.at[p], k.ly_r.at[p], k.lc_s.at[p], k.lc_r.at[p], done)
        next(steps)
        k.losses[p, g] = jnp.broadcast_to(
            jnp.sum(own_rows(mask, p) * (log_total - picked), axis=0, keepdims=True), (8, OWN)
        )
        done.extend(share_g(k.losses.at[p], k.lo_s.at[p], k.lo_r.at[p]))
        yield "lg"
        next(steps)
        yield "lgf"
        next(steps)
        yield "lgc"
        next(steps, None)

        def terms(xb):
            out = lax.dot_general(
                lg[xb].reshape(NZ * R, VOC),
                k.head[...],
                (((1,), (1,)), ((), ())),
                preferred_element_type=F32,
            )
            part[xb] = out.reshape(NZ, R, WIDE)

        final = []
        steps = reduce_tensor(part, bufs + sems(1), terms, done, final)
        next(steps)
        yield "r2a"
        next(steps)
        yield "r2x"
        next(steps)
        yield "r2b"
        next(steps, None)
        scaled = final[0] * gain_f
        unit = k.unit[p]
        own_inner = jnp.sum(scaled * unit, axis=1, keepdims=True)
        k.inners[p, g] = jnp.broadcast_to(own_inner, (R, OWN))
        sent = share_g(k.inners.at[p], k.sq_s.at[PARTS + p], k.sq_r.at[PARTS + p])
        yield "in"
        finish(sent)
        inner = jnp.sum(k.inners[p], axis=0)[:, :1] / D
        mg[x, z] = ((scaled - unit * inner) / mixed_rms).astype(BF16)
        steps = gather_tensor(mg, *agt(1), done)
        next(steps)
        yield "mg1"
        next(steps)
        yield "mg2"
        next(steps)
        yield "mgx"
        next(steps, None)
        nhg = k.nhg.at[p]
        nhg[...] = lax.dot_general(
            mg[...].reshape(TOK, WIDE),
            k.proj_h[...],
            (((1,), (1,)), ((), ())),
            preferred_element_type=F32,
        ).reshape(NG, GR, FEAT)
        sent = scatter_g(nhg, k.nhg_recv.at[p], k.ng_s.at[p], k.ng_r.at[p])
        k.nhg_recv[p, g] = nhg[g]
        yield "ng"
        arrive(sent)
        done.extend(sent)
        scaled = jnp.sum(k.nhg_recv[p], axis=0) * gain_h
        unit_rows = own_rows(k.sums[:, :FEAT], p)
        inner = jnp.sum(scaled * unit_rows, axis=1, keepdims=True)
        sent = share_tensor(
            to_tile([inner]), k.last_stats.at[p], k.ls_s.at[p], k.ls_r.at[p]
        )
        yield "ls"
        finish(sent)
        inner = to_col(jnp.sum(k.last_stats[p], axis=0)[:1, :], GR) / D
        hidden_grad = (scaled - unit_rows * inner) / own_rows(k.sums[:, FEAT : FEAT + 1], p)
        k.nhg_recv[p, 0] = hidden_grad

    def head_side():
        def tile(n, carry):
            columns = pl.ds(pl.multiple_of(n * 256, 256), 256)
            total = jnp.zeros((WIDE, 256), F32)
            for p in range(PARTS):
                total = total + jnp.dot(
                    k.flipped[p],
                    k.lg[p, :, :, :, columns].reshape(TOK, 256),
                    preferred_element_type=F32,
                )
            k.head_grad[:, columns] = total.astype(BF16)
            return carry

        lax.fori_loop(0, VOC // 256, tile, 0)
        yield

    def proj_side():
        for ref, out in ((k.nh, k.ph_grad), (k.ne, k.pe_grad)):
            total = jnp.zeros((FEAT, WIDE), F32)
            for p in range(PARTS):
                rows = ref[:, :, p * R : (p + 1) * R, :].reshape(TOK, FEAT)
                total = total + lax.dot_general(
                    rows,
                    k.mg[p].reshape(TOK, WIDE),
                    (((0,), (0,)), ((), ())),
                    preferred_element_type=F32,
                )
            out[...] = total.astype(BF16)
        yield

    flows = {"a": chain(0), "b": chain(1), "h": head_side(), "p": proj_side()}
    for step in SCHEDULE:
        name, label = step.split(".")
        for reached in flows[name]:
            if reached == label:
                break
    for one in done:
        one.wait_send()
    for p in range(PARTS):
        for i, (_, dev) in enumerate(g_peers()):
            rcopy(
                k.losses.at[p, g], k.losses.at[p, g], k.lo_s.at[p, i], k.lo_r.at[p, i], dev
            ).wait_recv()
    loss = k.losses[0]
    for p in range(1, PARTS):
        loss = loss + k.losses[p]
    k.loss[...] = jnp.sum(loss, axis=0)[:1, :1] / mask_total
    whole = jnp.concatenate(
        [k.nhg_recv[p, 0].reshape(4, R, FEAT) for p in range(PARTS)], axis=1
    ).reshape(OWN, FEAT)
    k.hidden_grad[...] = whole.T.astype(BF16)


SCHEDULE = (
    "a.rs1a",
    "a.rs1x",
    "b.rs1a",
    "a.rs1b",
    "b.rs1x",
    "a.sq",
    "b.rs1b",
    "a.ag1",
    "a.ag2",
    "b.sq",
    "a.agx",
    "b.ag1",
    "a.ry",
    "b.ag2",
    "b.agx",
    "a.ryx",
    "b.ry",
    "a.st",
    "b.ryx",
    "a.lg",
    "a.lgf",
    "b.st",
    "a.lgc",
    "b.lg",
    "a.r2a",
    "b.lgf",
    "a.r2x",
    "b.lgc",
    "a.r2b",
    "b.r2a",
    "h.end",
    "a.in",
    "b.r2x",
    "a.mg1",
    "a.mg2",
    "b.r2b",
    "a.mgx",
    "b.in",
    "b.mg1",
    "a.ng",
    "b.mg2",
    "b.mgx",
    "a.ls",
    "b.ng",
    "p.end",
    "b.ls",
    "a.end",
    "b.end",
)


def vmem(n):
    return [pl.BlockSpec(memory_space=pltpu.VMEM)] * n


def dma(*shape):
    return pltpu.SemaphoreType.DMA(shape)


def pairs(*shapes):
    return [dma(*shape) for shape in shapes for _ in range(2)]


def call(*args):
    return pl.pallas_call(
        kernel,
        out_shape=(
            jax.ShapeDtypeStruct((1, 1), F32),
            jax.ShapeDtypeStruct((FEAT, OWN), BF16),
            jax.ShapeDtypeStruct((FEAT, WIDE), BF16),
            jax.ShapeDtypeStruct((FEAT, WIDE), BF16),
            jax.ShapeDtypeStruct((WIDE, VOC), BF16),
        ),
        in_specs=vmem(7) + [pl.BlockSpec(memory_space=pl.ANY)] * 4,
        out_specs=tuple(vmem(5)),
        scratch_shapes=[
            pltpu.VMEM((FEAT, TABLE), BF16),
            pltpu.VMEM((FEAT, WIDE), BF16),
            pltpu.VMEM((FEAT, WIDE), BF16),
            pltpu.VMEM((WIDE, VOC), BF16),
            dma(4),
            pltpu.VMEM((NG, 8, OWN), F32),
            pltpu.VMEM((NG, 1, OWN), jnp.int32),
            pltpu.VMEM((NG * OWN, 1), jnp.int32),
            pltpu.VMEM((NG, OWN, FEAT), BF16),
            pltpu.VMEM((NG, OWN, FEAT), BF16),
            pltpu.VMEM((NX, NZ, ROWS, FEAT), BF16),
            pltpu.VMEM((NX, NZ, ROWS, FEAT), BF16),
            pltpu.VMEM((PARTS, R, WIDE), F32),
            pltpu.VMEM((PARTS, NX, NZ, R, WIDE), BF16),
            pltpu.VMEM((PARTS, NC, NY, GR, VOC), F32),
            pltpu.VMEM((PARTS, NY, GR, VOC), F32),
            pltpu.VMEM((PARTS, NY - 1, GR, VOC), F32),
            pltpu.VMEM((PARTS, NX, NZ, R, VOC), BF16),
            pltpu.VMEM((PARTS, WIDE, TOK), BF16),
            pltpu.VMEM((PARTS, NX, NZ, R, WIDE), BF16),
            pltpu.VMEM((PARTS, NG, GR, FEAT), F32),
            pltpu.VMEM((PARTS, NG, GR, FEAT), F32),
            pltpu.VMEM((OWN, 256), F32),
        ]
        + reduce_scratch()
        + [
            pltpu.VMEM((NT, 8, OWN), F32),
            pltpu.VMEM((NT, 8, OWN), F32),
            pltpu.VMEM((PARTS, NT, 8, OWN), F32),
            pltpu.VMEM((PARTS, NT, 8, OWN), F32),
            pltpu.VMEM((NG, 8, OWN), F32),
            pltpu.VMEM((PARTS, NG, 8, OWN), F32),
            pltpu.VMEM((PARTS, NG, R, OWN), F32),
            pltpu.VMEM((PARTS, NG, R, OWN), F32),
        ]
        + pairs((NG - 1,), (NG - 1,))
        + [pltpu.SemaphoreType.DMA] * 4
        + pairs((NG - 1,), (2, 4), (2, 4), (NG - 1,))
        + pairs((PARTS, 2, NZ), (PARTS, 2, NZ), (2 * PARTS, NG - 1))
        + pairs((PARTS, 2, NZ), (PARTS, 2, NZ))
        + pairs((PARTS, CHUNKS), (PARTS, 6), (PARTS,), (PARTS, NG - 1))
        + pairs((PARTS, 4), (PARTS, 4), (PARTS, NG - 1), (PARTS,)),
        compiler_params=pltpu.CompilerParams(
            collective_id=0, has_side_effects=True, vmem_limit_bytes=VMEM_LIMIT
        ),
        name="whole",
    )(*args)


def settle_kernel(a, b, c, d, a_out, b_out, c_out, d_out):
    @pl.when(pl.program_id(0) == 0)
    def _():
        a_out[...] = a[...]
        b_out[...] = b[...]
        c_out[...] = c[...]

    d_out[...] = d[...]


def settle(*arrays):
    blocks = 4
    specs = [pl.BlockSpec(a.shape, lambda i: (0, 0)) for a in arrays[:3]]
    specs.append(pl.BlockSpec((WIDE // blocks, VOC), lambda i: (i, 0)))
    return pl.pallas_call(
        settle_kernel,
        grid=(blocks,),
        out_shape=tuple(jax.ShapeDtypeStruct(a.shape, a.dtype) for a in arrays),
        in_specs=specs,
        out_specs=tuple(specs),
        compiler_params=pltpu.CompilerParams(vmem_limit_bytes=VMEM_LIMIT),
        name="settle",
    )(*arrays)


def per_device(
    hidden_prev,
    next_ids,
    targets,
    loss_mask,
    gain_hidden,
    gain_embed,
    gain_final,
    embed_table,
    proj_hidden,
    proj_embed,
    head_weight,
):
    loss, hidden_grad, ph_grad, pe_grad, head_grad = call(
        hidden_prev.T,
        next_ids[None, :],
        targets[None, :],
        loss_mask[None, :],
        gain_hidden,
        gain_embed,
        gain_final,
        embed_table.T,
        proj_hidden,
        proj_embed,
        head_weight,
    )
    hidden_grad, ph_grad, pe_grad, head_grad = settle(hidden_grad, ph_grad, pe_grad, head_grad)
    return (loss[0, 0], hidden_grad.T, ph_grad, pe_grad, head_grad)


def solution(mesh):
    return jax.shard_map(
        per_device,
        mesh=mesh,
        in_specs=(
            P(("context", "dp"), "tensor"),
            P(("context", "dp")),
            P(("context", "dp")),
            P(("context", "dp")),
            P("tensor"),
            P("tensor"),
            P(("context", "dp")),
            P(("context", "dp"), "tensor"),
            P("tensor", ("context", "dp")),
            P("tensor", ("context", "dp")),
            P(("context", "dp"), "tensor"),
        ),
        out_specs=(
            P(),
            P(("context", "dp"), "tensor"),
            P("tensor", ("context", "dp")),
            P("tensor", ("context", "dp")),
            P(("context", "dp"), "tensor"),
        ),
        check_vma=False,
    )
```

time: 984 us -> 263 us (0.27); the launches traced: 972 us -> 263 us
  waiting for transfers between devices: 508 us -> 0 us
  blocking collectives: 373 us -> 0 us
  Pallas kernels: 0 us -> 260 us
  matrix products: 39.1 us -> 0 us
  other arithmetic: 21.6 us -> 0 us
  between operations: 16.8 us -> 2.33 us
  local copies, waits for them, and re-layouts: 13.1 us -> 0 us
    psum x3 -> x0, waiting for transfers between devices: 371 us -> none  [the longest x1 157 us: per_device(): final_grad = lax.psum(final_terms, 'tensor')]
    pallas_call x0 -> x2, Pallas kernels: none -> 260 us  [the longest x1 255 us: call(): pl.pallas_call(kernel, out_shape=(jax.ShapeDtypeStruct((1, 1), F32), jax....]
    psum x6 -> x0, blocking collectives: 258 us -> none  [the longest x1 62 us: per_device(): embed_total = lax.psum(jnp.sum(embedded * embedded, axis=1), 'tensor')]
    reduce_scatter x2 -> x0, waiting for transfers between devices: 108 us -> none  [the longest x1 89.7 us: per_device(): lax.psum_scatter(jnp.dot(final_normed, head_weight, preferred_element_typ...]
    pmax x1 -> x0, blocking collectives: 61 us -> none  [per_device(): row_top = lax.pmax(local_top, 'tensor')]
    all_gather x2 -> x0, blocking collectives: 54.2 us -> none  [the longest x1 38.3 us: per_device(): lax.all_gather(own_hidden, ('context', 'dp'), axis=0, tiled=True)]
    dot_general x8 -> x0, matrix products: 39.1 us -> none  [the longest x1 10.9 us: per_device(): jnp.dot(final_normed, head_weight, preferred_element_type=jnp.float32)]
    all_gather x1 -> x0, waiting for transfers between devices: 28.6 us -> none  [per_device(): lax.all_gather(logit_grad, ('context', 'dp'), axis=0, tiled=True)]
  transfers between devices with their start and end apart: 6 -> 0, of which waited for: 6 -> 0; matrix products, arithmetic and copies ran while one was open for 1% -> 0% of each run, Pallas kernels for 0% -> 0%
where the time goes in v2:
time: 263 us
  Pallas kernels  260 us (99%)
    pallas_call x1, Pallas kernels, call(): pl.pallas_call(kernel, out_shape=(jax.ShapeDtypeStruct((1, 1), F32), jax....  255 us

profile of v2, /device:TPU:1, one launch (start us, length us, event | category | flops | bytes accessed | tf_op | source)
XLA Modules:
  0.0 262.5 jit_solution(942701125417150417)
XLA Ops:
  0.6 255.2 %whole.1 = (f32[1,1]{1,0:T(1,128)}, bf16[224,128]{1,0:T(8,128)(2,1)}, bf16[224,896]{1,0:T(8,128)(2,1)}, bf16[224,896]{1,0:T(8,128)(2,1)}, bf16[896,2048]{1,0:T(8,128)(2,1)}) custom-call(bf16[224,128]{1,0:T(8,128)(2,1)} %bitcast.8, s32[1,128]{1,0:T(1,128)} %bitcast.9, s32[1,128]{1,0:T(1,128)} %bitcast.10, s32[1,128]{1,0:T(1,128)} %bitcast.11, ...), custom_call_target="tpu_custom_call" | custom-call | tf_op jit(solution)/shard_map/whole/pallas_call | solution.py:791
  255.8 5.0 %settle.1 = (bf16[224,128]{1,0:T(8,128)(2,1)}, bf16[224,896]{1,0:T(8,128)(2,1)}, bf16[224,896]{1,0:T(8,128)(2,1)}, bf16[896,2048]{1,0:T(8,128)(2,1)}) custom-call(bf16[224,128]{1,0:T(8,128)(2,1)} %get-tuple-element.15.a, bf16[224,896]{1,0:T(8,128)(2,1)} %get-tuple-element.16.b, bf16[224,896]{1,0:T(8,128)(2,1)} %get-tuple-element.17.c, ...), custom_call_target="tpu_custom_call" | custom-call | tf_op jit(solution)/shard_map/settle/pallas_call | solution.py:866

commit v3 on v2

--- a/solution.py
+++ b/solution.py
@@ -683,21 +683,29 @@
             k.head_grad[:, columns] = total.astype(BF16)
             return carry
 
-        lax.fori_loop(0, VOC // 256, tile, 0)
+        lax.fori_loop(0, VOC // 512, tile, 0)
+        yield "half"
+        lax.fori_loop(VOC // 512, VOC // 256, tile, 0)
         yield
 
     def proj_side():
-        for ref, out in ((k.nh, k.ph_grad), (k.ne, k.pe_grad)):
-            total = jnp.zeros((FEAT, WIDE), F32)
-            for p in range(PARTS):
-                rows = ref[:, :, p * R : (p + 1) * R, :].reshape(TOK, FEAT)
-                total = total + lax.dot_general(
-                    rows,
-                    k.mg[p].reshape(TOK, WIDE),
-                    (((0,), (0,)), ((), ())),
-                    preferred_element_type=F32,
-                )
-            out[...] = total.astype(BF16)
+        def product(ref, p):
+            return lax.dot_general(
+                ref[:, :, p * R : (p + 1) * R, :].reshape(TOK, FEAT),
+                k.mg[p].reshape(TOK, WIDE),
+                (((0,), (0,)), ((), ())),
+                preferred_element_type=F32,
+            )
+
+        rows = FEAT // NY
+        for i, ref in enumerate((k.nh, k.ne)):
+            k.core_recv[0, :, :rows, i * WIDE : (i + 1) * WIDE] = product(ref, 0).reshape(
+                NY, rows, WIDE
+            )
+        yield "half"
+        for i, (ref, out) in enumerate(((k.nh, k.ph_grad), (k.ne, k.pe_grad))):
+            first = k.core_recv[0, :, :rows, i * WIDE : (i + 1) * WIDE].reshape(FEAT, WIDE)
+            out[...] = (first + product(ref, 1)).astype(BF16)
         yield
 
     flows = {"a": chain(0), "b": chain(1), "h": head_side(), "p": proj_side()}
@@ -754,16 +762,18 @@
     "b.lgc",
     "a.r2b",
     "b.r2a",
-    "h.end",
+    "h.half",
     "a.in",
     "b.r2x",
     "a.mg1",
+    "h.end",
     "a.mg2",
     "b.r2b",
     "a.mgx",
     "b.in",
     "b.mg1",
     "a.ng",
+    "p.half",
     "b.mg2",
     "b.mgx",
     "a.ls",

time: 263 us -> 262 us (level)
  no operation moved by 1% of the time
where the time goes in v3:
time: 262 us; the launch traced here: 261 us
  Pallas kernels  259 us (99%)
    pallas_call x1, Pallas kernels, call(): pl.pallas_call(kernel, out_shape=(jax.ShapeDtypeStruct((1, 1), F32), jax....  254 us

profile of v3, /device:TPU:1, one launch (start us, length us, event | category | flops | bytes accessed | tf_op | source)
XLA Modules:
  0.0 261.2 jit_solution(16387764201813009529)
XLA Ops:
  0.6 253.9 %whole.1 = (f32[1,1]{1,0:T(1,128)}, bf16[224,128]{1,0:T(8,128)(2,1)}, bf16[224,896]{1,0:T(8,128)(2,1)}, bf16[224,896]{1,0:T(8,128)(2,1)}, bf16[896,2048]{1,0:T(8,128)(2,1)}) custom-call(bf16[224,128]{1,0:T(8,128)(2,1)} %bitcast.8, s32[1,128]{1,0:T(1,128)} %bitcast.9, s32[1,128]{1,0:T(1,128)} %bitcast.10, s32[1,128]{1,0:T(1,128)} %bitcast.11, ...), custom_call_target="tpu_custom_call" | custom-call | tf_op jit(solution)/shard_map/whole/pallas_call | solution.py:801
  254.5 5.0 %settle.1 = (bf16[224,128]{1,0:T(8,128)(2,1)}, bf16[224,896]{1,0:T(8,128)(2,1)}, bf16[224,896]{1,0:T(8,128)(2,1)}, bf16[896,2048]{1,0:T(8,128)(2,1)}) custom-call(bf16[224,128]{1,0:T(8,128)(2,1)} %get-tuple-element.15.a, bf16[224,896]{1,0:T(8,128)(2,1)} %get-tuple-element.16.b, bf16[224,896]{1,0:T(8,128)(2,1)} %get-tuple-element.17.c, ...), custom_call_target="tpu_custom_call" | custom-call | tf_op jit(solution)/shard_map/settle/pallas_call | solution.py:876
